TPU v7x, 1024 devices: a whole 4x4x32 slice. The times are simulated.
1024 devices in a mesh: dp: 4 (over x), pipe: 8 (over y, core), ctx: 32 (over z).
Axes of the slice: x: 4, y: 4, z: 32, core: 2. Of those that a mesh axis runs over, the one named last changes fastest.
Arguments:
- activations: bfloat16 [4, 8, 3, 32, 262144], P('dp', 'pipe', None, None, 'ctx'), may hold values from -16 to 16
- cotangents: bfloat16 [4, 8, 32, 262144], P('dp', 'pipe', None, 'ctx'), may hold values from -3 to 3
- norm_gains: float32 [8, 2, 32, 64], P('pipe', None, 'ctx'), may hold values from 0.6 to 6.6
- key_blocks: int32 [8, 32, 32, 2], P('pipe', 'ctx'), may hold values from 0 to 32, as said below
Outputs:
- attended: bfloat16 [4, 8, 32, 262144], P('dp', 'pipe', None, 'ctx')
- gain_grads: float32 [8, 2, 32, 64], P('pipe', None, 'ctx')
Inputs may be any that keep to these rules, and one draw needn't show every extreme that they name: `key_blocks`: each row lists distinct key blocks and always its own block first; unused slots hold 32 and stand after the used ones; rows hold different numbers of blocks.
All inputs are finite; a program needn't handle non-finite values.
Results may differ from a plain program's by a relative error of at most 0.0035.
The roundings to bfloat16 on the way count: a program that leaves them out, or rounds other values in their place, can miss the bound.
Values may be sent and summed in bfloat16 or wider, within the bound.
A program may use at most 32 MiB of HBM per device.

v0:
```python
import math

import jax
import jax.numpy as jnp
from jax import lax
from jax.sharding import PartitionSpec as P

HEAD_DIM = 64
BLOCK = 128


EPS = 1e-06


def from_behind(value, axis, steps):
    count = lax.axis_size(axis)
    pairs = [(source, (source + steps) % count) for source in range(count)]
    return lax.ppermute(value, axis, pairs)


def normalize(raw_vals, gain_row):
    vals_f = raw_vals.astype(jnp.float32)
    unit_rows = vals_f * lax.rsqrt(jnp.mean(vals_f * vals_f, axis=-1, keepdims=True) + EPS)
    return (unit_rows, (unit_rows * gain_row).astype(jnp.bfloat16))


def gather_tiles(field_blocks, safe_idx):
    picked = jnp.take(field_blocks, safe_idx, axis=0)
    return picked.reshape(
        safe_idx.shape[0], safe_idx.shape[1] * field_blocks.shape[1], field_blocks.shape[2]
    )


def group_layout(block_count):
    group_size = math.gcd(block_count, max(1, 512 // BLOCK))
    return (group_size, block_count // group_size)


def masked_scores(q_part, k_blocks, row_lists):
    block_count = k_blocks.shape[0]
    live_slots = row_lists < block_count
    safe_idx = jnp.where(live_slots, row_lists, 0)
    k_tiles = gather_tiles(k_blocks, safe_idx)
    scores = jnp.einsum(
        "gqd,gkd->gqk", q_part, k_tiles, preferred_element_type=jnp.float32
    ) * HEAD_DIM ** (-0.5)
    key_mask = jnp.repeat(live_slots, BLOCK, axis=1)[:, None, :]
    return (jnp.where(key_mask, scores, -jnp.inf), safe_idx, k_tiles)


def forward_head(q_normed, k_normed, value_rows, block_list):
    block_count = block_list.shape[0]
    group_size, group_count = group_layout(block_count)
    q_blocks = q_normed.reshape(block_count, BLOCK, HEAD_DIM)
    k_blocks = k_normed.reshape(block_count, BLOCK, HEAD_DIM)
    v_blocks = value_rows.reshape(block_count, BLOCK, HEAD_DIM)

    def forward_one_group(group_idx):
        start = group_idx * group_size
        row_lists = lax.dynamic_slice_in_dim(block_list, start, group_size, 0)
        q_part = lax.dynamic_slice_in_dim(q_blocks, start, group_size, 0)
        scores, safe_idx, k_tiles = masked_scores(q_part, k_blocks, row_lists)
        row_max = jnp.max(scores, axis=-1, keepdims=True)
        exp_rows = jnp.exp(scores - row_max)
        row_sum = jnp.sum(exp_rows, axis=-1, keepdims=True)
        prob_rows = (exp_rows / row_sum).astype(jnp.bfloat16)
        v_tiles = gather_tiles(v_blocks, safe_idx)
        attended = jnp.einsum(
            "gqk,gkd->gqd", prob_rows, v_tiles, preferred_element_type=jnp.float32
        )
        return (attended, row_max, row_sum)

    attended, row_max, row_sum = lax.map(
        forward_one_group, jnp.arange(group_count, dtype=jnp.int32)
    )
    attended = attended.reshape(block_count, BLOCK, HEAD_DIM)
    return (
        attended.astype(jnp.bfloat16).reshape(block_count * BLOCK * HEAD_DIM),
        attended,
        row_max.reshape(block_count, BLOCK, 1),
        row_sum.reshape(block_count, BLOCK, 1),
    )


def backward_head(
    q_normed,
    k_normed,
    value_rows,
    q_unit,
    k_unit,
    grad_rows,
    block_list,
    attended_full,
    row_max,
    row_sum,
):
    block_count = block_list.shape[0]
    group_size, group_count = group_layout(block_count)
    q_blocks = q_normed.reshape(block_count, BLOCK, HEAD_DIM)
    k_blocks = k_normed.reshape(block_count, BLOCK, HEAD_DIM)
    v_blocks = value_rows.reshape(block_count, BLOCK, HEAD_DIM)
    q_unit_blocks = q_unit.reshape(block_count, BLOCK, HEAD_DIM)
    k_unit_blocks = k_unit.reshape(block_count, BLOCK, HEAD_DIM)
    grad_blocks = grad_rows.reshape(block_count, BLOCK, HEAD_DIM)

    def backward_one_group(totals, group_idx):
        start = group_idx * group_size
        row_lists = lax.dynamic_slice_in_dim(block_list, start, group_size, 0)
        q_part = lax.dynamic_slice_in_dim(q_blocks, start, group_size, 0)
        scores, safe_idx, k_tiles = masked_scores(q_part, k_blocks, row_lists)
        max_part = lax.dynamic_slice_in_dim(row_max, start, group_size, 0)
        sum_part = lax.dynamic_slice_in_dim(row_sum, start, group_size, 0)
        out_part = lax.dynamic_slice_in_dim(attended_full, start, group_size, 0)
        v_tiles = gather_tiles(v_blocks, safe_idx)
        grad_part = lax.dynamic_slice_in_dim(grad_blocks, start, group_size, 0)
        row_dot = jnp.sum(grad_part.astype(jnp.float32) * out_part, axis=-1, keepdims=True)
        grad_probs = jnp.einsum(
            "gqd,gkd->gqk", grad_part, v_tiles, preferred_element_type=jnp.float32
        )
        prob_rows = jnp.exp(scores - max_part) / sum_part
        grad_scores = (prob_rows * (grad_probs - row_dot) * HEAD_DIM ** (-0.5)).astype(jnp.bfloat16)
        grad_query = jnp.einsum(
            "gqk,gkd->gqd", grad_scores, k_tiles, preferred_element_type=jnp.float32
        )
        grad_key = jnp.einsum(
            "gqk,gqd->gkd", grad_scores, q_part, preferred_element_type=jnp.float32
        )
        unit_part = lax.dynamic_slice_in_dim(q_unit_blocks, start, group_size, 0)
        unit_tiles = gather_tiles(k_unit_blocks, safe_idx)
        query_total = totals[0] + jnp.sum(grad_query * unit_part, axis=(0, 1))
        key_total = totals[1] + jnp.sum(grad_key * unit_tiles, axis=(0, 1))
        return ((query_total, key_total), None)

    zero_row = jnp.zeros((HEAD_DIM,), jnp.float32)
    final_totals, unused_out = lax.scan(
        backward_one_group, (zero_row, zero_row), jnp.arange(group_count, dtype=jnp.int32)
    )
    return jnp.stack([final_totals[0], final_totals[1]])


def prepare(head_block, gain_pair):
    heads_here = head_block.shape[1]
    seq_len = head_block.shape[2] // HEAD_DIM
    fields = head_block.reshape(3, heads_here, seq_len, HEAD_DIM)
    q_unit, q_normed = normalize(fields[0], gain_pair[0][:, None, :])
    k_unit, k_normed = normalize(fields[1], gain_pair[1][:, None, :])
    return (q_unit, q_normed, k_unit, k_normed, fields[2])


def local(activations, cotangents, norm_gains, key_blocks):
    section_block = activations[0, 0]
    section_grad = cotangents[0, 0][None]
    gain_pair = norm_gains[0]
    block_table = key_blocks[0]
    arrived = from_behind(section_block, "pipe", 1)
    returned = from_behind(section_grad, "pipe", -1)
    head_block, head_grad = (
        lax.all_to_all(arrived, "ctx", split_axis=1, concat_axis=2, tiled=True),
        lax.all_to_all(returned, "ctx", split_axis=1, concat_axis=2, tiled=True),
    )
    prepared = prepare(head_block, gain_pair)
    forward_out = jax.vmap(forward_head)(prepared[1], prepared[3], prepared[4], block_table)
    attended_heads, attended_full, row_max, row_sum = forward_out
    attended = lax.all_to_all(attended_heads, "ctx", split_axis=1, concat_axis=0, tiled=True)
    heads_here = head_grad.shape[1]
    grad_fields = head_grad[0].reshape(heads_here, head_grad.shape[2] // HEAD_DIM, HEAD_DIM)
    head_terms = jax.vmap(backward_head)(
        prepared[1],
        prepared[3],
        prepared[4],
        prepared[0],
        prepared[2],
        grad_fields,
        block_table,
        attended_full,
        row_max,
        row_sum,
    )
    local_grads = jnp.transpose(head_terms, (1, 0, 2))
    summed = lax.psum(local_grads, "dp")
    return (attended[None, None], summed[None])


def solution(mesh):
    return jax.shard_map(
        local,
        mesh=mesh,
        in_specs=(
            P("dp", "pipe", None, None, "ctx"),
            P("dp", "pipe", None, "ctx"),
            P("pipe", None, "ctx", None),
            P("pipe", "ctx", None, None),
        ),
        out_specs=(P("dp", "pipe", None, "ctx"), P("pipe", None, "ctx", None)),
        check_vma=False,
    )
```

profile of v0, /device:TPU:24, one launch (start us, length us, event | category | flops | bytes accessed | tf_op | source)
XLA Modules:
  0.0 535.0 jit_solution(12836391318954260537)
XLA Ops:
  0.8 7.0 %collective-permute-done.1 = bf16[1,32,8192]{2,1,0:T(8,128)(2,1)S(1)} collective-permute-done((bf16[1,32,8192]{2,1,0:T(8,128)(2,1)}, bf16[1,32,8192]{2,1,0:T(8,128)(2,1)S(1)}, u32[]{:S(2)}, u32[]{:S(2)}) %collective-permute-start.1) | collective-permute-done | bytes 524320 | tf_op jit(solution)/shard_map/ppermute | solution.py:18
  9.5 3.7 reduce.26
  14.4 28.7 %all-to-all-start.2 = ((bf16[32,2,4096]{2,1,0:T(2,128)(2,1)}), bf16[32,2,4096]{2,1,0:T(2,128)(2,1)S(1)}, u32[]{:S(2)}, u32[]{:S(2)}) async-start(bf16[32,2,4096]{2,1,0:T(2,128)(2,1)} %reshape.819), calls=%async_computation.2 | async-start | bytes 1048576 | tf_op jit(solution)/shard_map/all_to_all | solution.py:159
  43.1 2.4 collective-permute-start
  45.5 17.5 %collective-permute-done = bf16[3,32,8192]{2,1,0:T(8,128)(2,1)S(1)} collective-permute-done((bf16[3,32,8192]{2,1,0:T(8,128)(2,1)S(1)}, bf16[3,32,8192]{2,1,0:T(8,128)(2,1)S(1)}, u32[]{:S(2)}, u32[]{:S(2)}) %collective-permute-start) | collective-permute-done | bytes 1572896 | tf_op jit(solution)/shard_map/ppermute | solution.py:18
  63.0 2.7 copy.181
  65.7 42.5 %all-to-all-done.2 = bf16[32,2,4096]{2,1,0:T(2,128)(2,1)S(1)} async-done(((bf16[32,2,4096]{2,1,0:T(2,128)(2,1)}), bf16[32,2,4096]{2,1,0:T(2,128)(2,1)S(1)}, u32[]{:S(2)}, u32[]{:S(2)}) %all-to-all-start.2) | async-done | bytes 524320 | tf_op jit(solution)/shard_map/all_to_all | solution.py:159
  109.0 4.5 all-to-all-start
  113.6 3.6 reshape.820
  117.2 3.9 bitcast_reduce_fusion
  124.3 181.6 %all-to-all-done = bf16[3,32,8192]{2,0,1:T(4,128)(2,1)S(1)} async-done(((bf16[3,32,8192]{2,0,1:T(4,128)(2,1)}), bf16[3,32,8192]{2,0,1:T(4,128)(2,1)S(1)}, u32[]{:S(2)}, u32[]{:S(2)}) %all-to-all-start) | async-done | bytes 1572896 | tf_op jit(solution)/shard_map/all_to_all | solution.py:158
  305.8 12.3 %multiply_reduce_fusion = (f32[32,8192]{1,0:T(8,128)}, f32[32,8192]{1,0:T(8,128)}, f32[32,8192]{1,0:T(8,128)S(1)}, f32[32,8192]{1,0:T(8,128)}) fusion(bf16[3,32,8192]{2,0,1:T(4,128)(2,1)S(1)} %all-to-all-done), kind=kLoop, calls=%fused_computation.101 | loop fusion | flops 1048576 | bytes 5242880 | tf_op jit(solution)/shard_map/mul | solution.py:23
  318.1 3.3 mul.171
  321.4 2.2 reduce_sum.59
  323.6 3.1 mul.164
  326.7 2.2 reduce_sum.58
  329.0 3.1 reshape.718
  334.2 4.5 multiply_convert_fusion
  338.7 2.4 copy.182
  341.0 3.9 slice_reduce_fusion
  347.0 47.3 %while.36 = (s32[]{:T(128)}, f32[8,1,4,128,64]{3,4,2,1,0:T(8,128)}, f32[8,1,4,128,1]{3,2,4,1,0:T(4,128)S(1)}, f32[8,1,4,128,1]{3,2,4,1,0:T(4,128)S(1)}, s32[8]{0...) while((s32[]{:T(128)}, f32[8,1,4,128,64]{3,4,2,1,0:T(8,128)}, ...), condition=%wide.region_5.7_spmd, body=%wide.region_2.6_spmd.sunk | while | flops 34733208 | bytes 3102015 | solution.py:73
  394.3 3.2 copy.188
  400.2 4.0 convert_element_type.141
  404.1 4.5 reduce.25
  408.7 2.2 reshape.817
  410.9 12.1 %all-to-all-start.1 = ((bf16[32,2,4096]{2,1,0:T(2,128)(2,1)}), bf16[32,2,4096]{2,1,0:T(2,128)(2,1)}, u32[]{:S(2)}, u32[]{:S(2)}) async-start(bf16[32,2,4096]{2,1,0:T(2,128)(2,1)} %reshape.817), calls=%async_computation.1 | async-start | bytes 1048576 | tf_op jit(solution)/shard_map/all_to_all | solution.py:164
  423.0 95.7 %while.37 = (s32[]{:T(128)}, f32[1,64]{1,0:T(1,128)S(1)}, f32[1,64]{1,0:T(1,128)S(1)}, s32[8]{0:T(128)S(1)}, s32[1,32,2]{1,2,0:T(2,128)S(1)}, /*index=5*/bf16[1,...) while((s32[]{:T(128)}, f32[1,64]{1,0:T(1,128)S(1)}, ...), condition=%wide.region_10.12_spmd.clone, body=%wide.region_6.11_spmd.clone.sunk | while | flops 68648872 | bytes 5135738 | solution.py:135
  430.1 2.2 gather_fusion.4
  442.1 2.2 gather_fusion.4
  454.0 2.2 gather_fusion.4
  518.7 11.0 %psum.7 = f32[1,2,1,64]{3,1,2,0:T(2,128)} all-reduce(f32[1,2,1,64]{3,1,2,0:T(2,128)S(1)} %bitcast.292), channel_id=1, replica_groups=mesh['dp'=4,'pipe'=8,'ctx'=32] {'dp'}, use_global_device_ids=true, to_apply=%region_11.13 | all-reduce | flops 128 | bytes 1024 | tf_op jit(solution)/shard_map/psum | solution.py:180
  529.8 3.6 reshape.818
  (404 shorter events, 140.2 us)
Async XLA Ops:
  0.6 7.2 %collective-permute-start.1 = (bf16[1,32,8192]{2,1,0:T(8,128)(2,1)}, bf16[1,32,8192]{2,1,0:T(8,128)(2,1)S(1)}, u32[]{:S(2)}, u32[]{:S(2)}) collective-permute-start(bf16[1,32,8192]{2,1,0:T(8,128)(2,1)} %bitcast.295), channel_id=1, source_target_pairs={{0,224},{32,0},{64,32},{96,64},{128,96},{160,128},{192,160},{224,1... | collective-permute-start | bytes 1572872 | tf_op jit(solution)/shard_map/ppermute | solution.py:18
  9.0 34.2 %copy-start.3 = (bf16[1,1,3,32,8192]{4,3,2,1,0:T(8,128)(2,1)S(1)}, bf16[1,1,3,32,8192]{4,3,2,1,0:T(8,128)(2,1)}, u32[]{:S(2)}) copy-start(bf16[1,1,3,32,8192]{4,3,2,1,0:T(8,128)(2,1)} %param.10) | copy-start | bytes 4718596
  14.4 93.9 %all-to-all-start.2 = ((bf16[32,2,4096]{2,1,0:T(2,128)(2,1)}), bf16[32,2,4096]{2,1,0:T(2,128)(2,1)S(1)}, u32[]{:S(2)}, u32[]{:S(2)}) async-start(bf16[32,2,4096]{2,1,0:T(2,128)(2,1)} %reshape.819), calls=%async_computation.2 | async-start | bytes 1048576 | tf_op jit(solution)/shard_map/all_to_all | solution.py:159
  43.1 19.9 %collective-permute-start = (bf16[3,32,8192]{2,1,0:T(8,128)(2,1)S(1)}, bf16[3,32,8192]{2,1,0:T(8,128)(2,1)S(1)}, u32[]{:S(2)}, u32[]{:S(2)}) collective-permute-start(bf16[3,32,8192]{2,1,0:T(8,128)(2,1)S(1)} %bitcast.294), channel_id=1, source_target_pairs={{0,32},{32,64},{64,96},{96,128},{128,160},{160,192},{192,224},{224... | collective-permute-start | bytes 4718600 | tf_op jit(solution)/shard_map/ppermute | solution.py:18
  65.7 47.9 %copy-start.2 = (f32[1,2,1,64]{3,2,1,0:T(1,128)S(1)}, f32[1,2,1,64]{3,2,1,0:T(1,128)}, u32[]{:S(2)}) copy-start(f32[1,2,1,64]{3,2,1,0:T(1,128)} %param.12) | copy-start | bytes 1540
  108.2 0.8 copy-start
  109.0 196.8 %all-to-all-start = ((bf16[3,32,8192]{2,0,1:T(4,128)(2,1)}), bf16[3,32,8192]{2,0,1:T(4,128)(2,1)S(1)}, u32[]{:S(2)}, u32[]{:S(2)}) async-start(bf16[3,32,8192]{2,0,1:T(4,128)(2,1)} %copy.181), calls=%async_computation | async-start | bytes 4194304 | tf_op jit(solution)/shard_map/all_to_all | solution.py:158
  338.7 8.3 %copy-start.1 = (s32[1,1,32,2]{2,3,1,0:T(2,128)S(1)}, s32[1,1,32,2]{2,3,1,0:T(2,128)}, u32[]{:S(2)}) copy-start(s32[1,1,32,2]{2,3,1,0:T(2,128)} %param.13) | copy-start | bytes 772
  410.9 118.9 %all-to-all-start.1 = ((bf16[32,2,4096]{2,1,0:T(2,128)(2,1)}), bf16[32,2,4096]{2,1,0:T(2,128)(2,1)}, u32[]{:S(2)}, u32[]{:S(2)}) async-start(bf16[32,2,4096]{2,1,0:T(2,128)(2,1)} %reshape.817), calls=%async_computation.1 | async-start | bytes 1048576 | tf_op jit(solution)/shard_map/all_to_all | solution.py:164
where the time goes:
time: 543 us; the launch traced here: 535 us
  waiting for transfers between devices  249 us (46%)
  local copies, waits for them, and re-layouts  109 us (20%)
  matrix products  56.9 us (10%)
  other arithmetic  49.4 us (9%)
  starting transfers between devices  47.9 us (9%)
  loops' own time  11.5 us (2%)
  blocking collectives  11 us (2%)
    all_to_all x1, waiting for transfers between devices, local(): lax.all_to_all(arrived, 'ctx', split_axis=1, concat_axis=2, tiled=True)  182 us
    all_to_all x1, waiting for transfers between devices, local(): lax.all_to_all(returned, 'ctx', split_axis=1, concat_axis=2, tiled=True)  42.5 us
    gather x120, local copies, waits for them, and re-layouts, gather_tiles(): picked = jnp.take(field_blocks, safe_idx, axis=0)  42.4 us
    all_to_all x1, starting transfers between devices, local(): lax.all_to_all(returned, 'ctx', split_axis=1, concat_axis=2, tiled=True)  28.7 us
    ppermute x2, waiting for transfers between devices, from_behind(): return lax.ppermute(value, axis, pairs)  24.5 us
    dot_general x16, matrix products, masked_scores(): jnp.einsum('gqd,gkd->gqk', q_part, k_tiles, preferred_element_type=jnp.fl...  19.5 us
    unnamed x16, local copies, waits for them, and re-layouts  17.7 us
    mul x1, other arithmetic, normalize(): vals_f * vals_f  12.3 us
  transfers between devices with their start and end apart: 5, of which 4 were waited for; matrix products, arithmetic and copies ran while one was open for 19% of the time, Pallas kernels for 0%

commit v1 on v0

v1 whole, which is shorter than its diff:
```python
import jax
import jax.numpy as jnp
from jax import lax
from jax.experimental import pallas as pl
from jax.experimental.pallas import tpu as pltpu
from jax.sharding import PartitionSpec as P

HEADS = 32
DIM = 64
BLOCKS = 32
ROWS = 64
EPS = 1e-06
F32 = jnp.float32
BF16 = jnp.bfloat16


def from_behind(value, axis, steps):
    count = lax.axis_size(axis)
    pairs = [(source, (source + steps) % count) for source in range(count)]
    return lax.ppermute(value, axis, pairs)


def dims_by_tokens(pairs):
    turned = pairs.astype(F32).T
    return jnp.concatenate([turned[:DIM], turned[DIM:]], axis=1)


def rows_of_pairs(turned):
    return jnp.concatenate([turned[:, :DIM], turned[:, DIM:]], axis=0).T


def contract(left, right, left_dim, right_dim):
    return lax.dot_general(
        left, right, (((left_dim,), (right_dim,)), ((), ())), preferred_element_type=F32
    )


def unit(vals):
    return vals * lax.rsqrt(jnp.mean(vals * vals, axis=0, keepdims=True) + EPS)


def one_head(query, key, value, grad, other_key, other_value, gain_row, live_row):
    scale = DIM ** (-0.5)
    gains = jnp.broadcast_to(gain_row, (2 * DIM, 2 * DIM)).T
    query_gain, key_gain = gains[:DIM], gains[DIM:]
    q_unit = unit(dims_by_tokens(query))
    k_unit = unit(dims_by_tokens(key))
    o_unit = unit(dims_by_tokens(other_key))
    q_normed = (q_unit * query_gain).astype(BF16)
    k_normed = jnp.concatenate([k_unit * key_gain, o_unit * key_gain], axis=1).astype(BF16)
    values = jnp.concatenate(
        [dims_by_tokens(value), dims_by_tokens(other_value)], axis=1
    ).astype(BF16)
    grad_f = dims_by_tokens(grad)
    scores = contract(k_normed, q_normed, 0, 0) * scale
    own_scores = scores[:128]
    other_scores = jnp.where(live_row > 0.5, scores[128:], -jnp.inf)
    row_max = jnp.maximum(
        jnp.max(own_scores, axis=0, keepdims=True), jnp.max(other_scores, axis=0, keepdims=True)
    )
    exp_own = jnp.exp(own_scores - row_max)
    exp_other = jnp.exp(other_scores - row_max)
    row_sum = jnp.sum(exp_own, axis=0, keepdims=True) + jnp.sum(exp_other, axis=0, keepdims=True)
    probs = jnp.concatenate([exp_own, exp_other], axis=0) / row_sum
    attended = contract(values, probs.astype(BF16), 1, 0)
    grad_probs = contract(values, grad_f.astype(BF16), 0, 0)
    row_dot = jnp.sum(grad_f * attended, axis=0, keepdims=True)
    grad_scores = (probs * (grad_probs - row_dot) * scale).astype(BF16)
    grad_query = contract(k_normed, grad_scores, 1, 0)
    grad_key = contract(q_normed, grad_scores, 1, 1)
    query_col = jnp.sum(grad_query * q_unit, axis=1, keepdims=True)
    key_col = jnp.sum(
        grad_key[:, :128] * k_unit + grad_key[:, 128:] * o_unit, axis=1, keepdims=True
    )
    return rows_of_pairs(attended).astype(BF16), jnp.concatenate([query_col, key_col], axis=0)


def attention_kernel(qkv_ref, grad_ref, other_ref, gain_ref, live_ref, out_ref, gain_out_ref):
    lane = lax.broadcasted_iota(jnp.int32, (2 * DIM, 128), 1)

    def step(head, totals):
        out, col = one_head(
            qkv_ref[0, head],
            qkv_ref[1, head],
            qkv_ref[2, head],
            grad_ref[head],
            other_ref[head, 0],
            other_ref[head, 1],
            gain_ref[head],
            live_ref[head],
        )
        out_ref[head] = out
        return jnp.where(lane == head, col, totals)

    totals = lax.fori_loop(0, HEADS, step, jnp.zeros((2 * DIM, 128), F32))
    gain_out_ref[...] = totals.T[:HEADS]


def attention(qkv, grads, others, gains, live):
    return pl.pallas_call(
        attention_kernel,
        out_shape=(
            jax.ShapeDtypeStruct((HEADS, ROWS, 128), BF16),
            jax.ShapeDtypeStruct((HEADS, 128), F32),
        ),
        in_specs=[pl.BlockSpec(memory_space=pltpu.VMEM)] * 5,
        out_specs=(pl.BlockSpec(memory_space=pltpu.VMEM),) * 2,
        compiler_params=pltpu.CompilerParams(vmem_limit_bytes=24 * 2**20),
    )(qkv, grads, others, gains, live)


def local(activations, cotangents, norm_gains, key_blocks):
    qkv = from_behind(activations[0, 0].reshape(3, HEADS, ROWS, 128), "pipe", 1)
    grads = from_behind(cotangents[0, 0].reshape(HEADS, ROWS, 128), "pipe", -1)
    table = key_blocks[0, 0]
    gain_rows = lax.all_gather(norm_gains[0].reshape(1, 1, 128), "ctx", axis=0, tiled=True)
    lists = lax.all_gather(table[None, :, 1], "ctx", axis=0, tiled=True)
    live = (lists[:, lax.axis_index("ctx")] < BLOCKS).astype(F32)
    live_rows = jnp.broadcast_to(live[:, None, None], (HEADS, 1, 128))
    keys_values = jnp.swapaxes(qkv[1:], 0, 1)
    held = lax.all_to_all(keys_values, "ctx", split_axis=0, concat_axis=0, tiled=True)
    listed = jnp.where(table[:, 1] < BLOCKS, table[:, 1], 0)
    picked = jnp.take(held, listed, axis=0)
    others = lax.all_to_all(picked, "ctx", split_axis=0, concat_axis=0, tiled=True)
    out, terms = attention(qkv, grads, others, gain_rows, live_rows)
    summed = lax.psum(lax.psum_scatter(terms, "ctx", scatter_dimension=0, tiled=True), "dp")
    return out.reshape(1, 1, HEADS, ROWS * 128), summed.reshape(1, 2, 1, DIM)


def solution(mesh):
    return jax.shard_map(
        local,
        mesh=mesh,
        in_specs=(
            P("dp", "pipe", None, None, "ctx"),
            P("dp", "pipe", None, "ctx"),
            P("pipe", None, "ctx", None),
            P("pipe", "ctx", None, None),
        ),
        out_specs=(P("dp", "pipe", None, "ctx"), P("pipe", None, "ctx", None)),
        check_vma=False,
    )
```

time: 543 us -> 566 us (1.042)
  blocking collectives: 11 us -> 355 us
  waiting for transfers between devices: 249 us -> 123 us
  local copies, waits for them, and re-layouts: 109 us -> 11.9 us
  matrix products: 56.9 us -> 0 us
  other arithmetic: 49.4 us -> 1.84 us
  Pallas kernels: 0 us -> 31.1 us
  loops' own time: 11.5 us -> 0 us
  starting transfers between devices: 47.9 us -> 36.9 us
    unnamed x0 -> x2, blocking collectives: none -> 292 us
    all_to_all x3 -> x2, waiting for transfers between devices: 224 us -> 104 us  [the longest x1 104 us: local(): lax.all_to_all(keys_values, 'ctx', split_axis=0, concat_axis=0, tiled=True)]
    dot_general x48 -> x0, matrix products: 56.9 us -> none  [the longest x16 19.5 us: masked_scores(): jnp.einsum('gqd,gkd->gqk', q_part, k_tiles, preferred_element_type=jnp.fl...]
    all_gather x0 -> x1, blocking collectives: none -> 52.8 us  [local(): lax.all_gather(norm_gains[0].reshape(1, 1, 128), 'ctx', axis=0, tiled=True)]
    gather x120 -> x1, local copies, waits for them, and re-layouts: 42.4 us -> 1.97 us  [local(): picked = jnp.take(held, listed, axis=0)]
    pallas_call x0 -> x1, Pallas kernels: none -> 31.1 us  [attention(): pl.pallas_call(attention_kernel, out_shape=(jax.ShapeDtypeStruct((HEADS,...]
    reduce_sum x18 -> x0, other arithmetic: 14.3 us -> none  [the longest x8 7.78 us: backward_one_group(): jnp.sum(grad_part.astype(jnp.float32) * out_part, axis=-1, keepdims=True)]
    mul x1 -> x0, other arithmetic: 12.3 us -> none  [normalize(): vals_f * vals_f]
  transfers between devices with their start and end apart: 5 -> 4, of which waited for: 4 -> 2; matrix products, arithmetic and copies ran while one was open for 19% -> 1% of each run, Pallas kernels for 0% -> 0%
where the time goes in v1:
time: 566 us; the launch traced here: 562 us
  blocking collectives  355 us (63%)
  waiting for transfers between devices  123 us (22%)
  starting transfers between devices  36.9 us (7%)
  Pallas kernels  31.1 us (5%)
  local copies, waits for them, and re-layouts  11.9 us (2%)
    unnamed x2, blocking collectives  292 us
    all_to_all x1, waiting for transfers between devices, local(): lax.all_to_all(keys_values, 'ctx', split_axis=0, concat_axis=0, tiled=True)  104 us
    all_gather x1, blocking collectives, local(): lax.all_gather(norm_gains[0].reshape(1, 1, 128), 'ctx', axis=0, tiled=True)  52.8 us
    pallas_call x1, Pallas kernels, attention(): pl.pallas_call(attention_kernel, out_shape=(jax.ShapeDtypeStruct((HEADS,...  31.1 us
    all_to_all x1, starting transfers between devices, local(): lax.all_to_all(keys_values, 'ctx', split_axis=0, concat_axis=0, tiled=True)  29 us
    ppermute x2, waiting for transfers between devices, from_behind(): return lax.ppermute(value, axis, pairs)  19.8 us
  transfers between devices with their start and end apart: 4, of which 2 were waited for; matrix products, arithmetic and copies ran while one was open for 1% of the time, Pallas kernels for 0%

profile of v1, /device:TPU:24, one launch (start us, length us, event | category | flops | bytes accessed | tf_op | source)
XLA Modules:
  0.0 562.0 jit_solution(2120180595921065163)
XLA Ops:
  0.6 1.8 copy.12
  2.5 0.0 collective-permute-start
  2.5 19.8 %collective-permute-done.qkv_ref = bf16[3,32,64,128]{3,2,1,0:T(8,128)(2,1)S(1)} collective-permute-done((bf16[3,32,64,128]{3,2,1,0:T(8,128)(2,1)S(1)}, bf16[3,32,64,128]{3,2,1,0:T(8,128)(2,1)S(1)}, u32[]{:S(2)}, u32[]{:S(2)}) %collective-permute-start) | collective-permute-done | bytes 1572896 | tf_op jit(solution)/shard_map/ppermute | solution.py:20
  22.3 0.1 slice_bitcast_fusion
  22.4 1.1 copy.9
  23.5 29.0 %all-to-all-start = ((bf16[32,2,64,128]{3,2,1,0:T(8,128)(2,1)}), bf16[32,2,64,128]{3,2,1,0:T(8,128)(2,1)}, u32[]{:S(2)}, u32[]{:S(2)}) async-start(bf16[32,2,64,128]{3,2,1,0:T(8,128)(2,1)} %copy.9), calls=%async_computation | async-start | bytes 2097152 | tf_op jit(solution)/shard_map/all_to_all | solution.py:121
  52.6 103.7 %all-to-all-done = bf16[32,2,64,128]{3,2,1,0:T(8,128)(2,1)} async-done(((bf16[32,2,64,128]{3,2,1,0:T(8,128)(2,1)}), bf16[32,2,64,128]{3,2,1,0:T(8,128)(2,1)}, u32[]{:S(2)}, u32[]{:S(2)}) %all-to-all-start) | async-done | bytes 1048608 | tf_op jit(solution)/shard_map/all_to_all | solution.py:121
  156.2 2.0 gather_fusion
  158.2 1.2 broadcast_select_fusion
  159.4 6.9 %all-to-all-start.1 = ((bf16[32,2,64,128]{3,2,1,0:T(8,128)(2,1)}), bf16[32,2,64,128]{3,2,1,0:T(8,128)(2,1)S(1)}, u32[]{:S(2)}, u32[]{:S(2)}) async-start(bf16[32,2,64,128]{3,2,1,0:T(8,128)(2,1)} %broadcast_select_fusion), calls=%async_computation.1 | async-start | bytes 2097152 | tf_op jit(solution)/shard_map/all_to_all | solution.py:124
  166.3 0.9 copy.13
  167.2 1.0 collective-permute-start.1
  168.1 1.4 fusion.1
  170.2 0.1 bitcast_dynamic-update-slice_fusion
  170.3 0.1 reshape.37
  170.4 0.1 copy.10
  170.5 0.5 broadcast.36
  171.0 0.0 copy-done.2
  171.0 0.7 reduce.7
  171.7 0.1 reshape_squeeze.11
  171.8 186.5 %all-reduce.1 = s32[32,32]{0,1:T(8,128)S(1)} all-reduce(s32[32,32]{0,1:T(8,128)S(1)} %copy.10), channel_id=2, replica_groups=mesh['dp'=4,'pipe'=8,'ctx'=32] {'ctx'}, use_global_device_ids=true, to_apply=%add | all-reduce | flops 1024 | bytes 8192
  358.2 52.8 %all_gather.6.gain_ref = f32[32,1,128]{2,1,0:T(1,128)S(1)} all-gather(f32[1,1,128]{2,1,0:T(1,128)S(1)} %reshape_squeeze.11), channel_id=1, replica_groups=mesh['dp'=4,'pipe'=8,'ctx'=32] {'ctx'}, dimensions={0}, use_global_device_ids=true | all-gather | bytes 16896 | tf_op jit(solution)/shard_map/all_gather | solution.py:116
  411.1 0.0 collective-permute-done.1.grad_ref
  411.1 0.0 all-to-all-done.1.other_ref
  411.1 0.1 broadcast_in_dim.23.live_ref
  411.2 31.1 %shard_map.59 = (bf16[32,64,128]{2,1,0:T(8,128)(2,1)S(1)}, f32[32,128]{1,0:T(8,128)S(1)}) custom-call(bf16[3,32,64,128]{3,2,1,0:T(8,128)(2,1)S(1)} %collective-permute-done.qkv_ref, bf16[32,64,128]{2,1,0:T(8,128)(2,1)S(1)} %collective-permute-done.1.grad_ref, bf16[32,2,64,128]{3,2,1,0:T(8,128)(2,1)S(1)} %all-to-all-done.1.other_ref, ...), custom_call_target="tpu_custom_call" | custom-call | tf_op jit(solution)/shard_map/pallas_call | solution.py:100
  442.3 0.8 copy-done
  443.1 105.1 %all-reduce.2 = f32[32,128]{1,0:T(8,128)S(1)} all-reduce(f32[32,128]{1,0:T(8,128)S(1)} %get-tuple-element.5), channel_id=3, replica_groups=mesh['dp'=4,'pipe'=8,'ctx'=32] {'ctx'}, use_global_device_ids=true, to_apply=%region_0.1.clone | all-reduce | flops 4096 | bytes 32768
  548.2 0.7 dynamic-slice_reduce_fusion
  548.9 0.1 reshape.27
  549.0 11.0 %psum.7 = f32[1,2,1,64]{3,1,2,0:T(2,128)} all-reduce(f32[1,2,1,64]{3,1,2,0:T(2,128)S(1)} %reshape.27), channel_id=1, replica_groups=mesh['dp'=4,'pipe'=8,'ctx'=32] {'dp'}, use_global_device_ids=true, to_apply=%region_1.2 | all-reduce | flops 128 | bytes 1024 | tf_op jit(solution)/shard_map/psum | solution.py:126
  560.0 2.1 reshape.26
  (10 shorter events, 0.0 us)
Async XLA Ops:
  2.5 19.9 %collective-permute-start = (bf16[3,32,64,128]{3,2,1,0:T(8,128)(2,1)S(1)}, bf16[3,32,64,128]{3,2,1,0:T(8,128)(2,1)S(1)}, u32[]{:S(2)}, u32[]{:S(2)}) collective-permute-start(bf16[3,32,64,128]{3,2,1,0:T(8,128)(2,1)S(1)} %bitcast.23), channel_id=1, source_target_pairs={{0,32},{32,64},{64,96},{96,128},{128,160},{160,192},{192,224},{224... | collective-permute-start | bytes 4718600 | tf_op jit(solution)/shard_map/ppermute | solution.py:20
  23.5 29.0 %copy-start.3 = (s32[1,1,32,2]{2,3,1,0:T(2,128)S(1)}, s32[1,1,32,2]{2,3,1,0:T(2,128)}, u32[]{:S(2)}) copy-start(s32[1,1,32,2]{2,3,1,0:T(2,128)} %param.7) | copy-start | bytes 772
  23.5 132.7 %all-to-all-start = ((bf16[32,2,64,128]{3,2,1,0:T(8,128)(2,1)}), bf16[32,2,64,128]{3,2,1,0:T(8,128)(2,1)}, u32[]{:S(2)}, u32[]{:S(2)}) async-start(bf16[32,2,64,128]{3,2,1,0:T(8,128)(2,1)} %copy.9), calls=%async_computation | async-start | bytes 2097152 | tf_op jit(solution)/shard_map/all_to_all | solution.py:121
  159.4 6.9 %copy-start.1 = (bf16[1,1,32,8192]{3,2,1,0:T(8,128)(2,1)S(1)}, bf16[1,1,32,8192]{3,2,1,0:T(8,128)(2,1)}, u32[]{:S(2)}) copy-start(bf16[1,1,32,8192]{3,2,1,0:T(8,128)(2,1)} %param.5) | copy-start | bytes 1572868
  159.4 11.7 %copy-start.2 = (f32[1,2,1,64]{3,2,1,0:T(1,128)S(1)}, f32[1,2,1,64]{3,2,1,0:T(1,128)}, u32[]{:S(2)}) copy-start(f32[1,2,1,64]{3,2,1,0:T(1,128)} %param.6) | copy-start | bytes 1540
  159.4 251.7 %all-to-all-start.1 = ((bf16[32,2,64,128]{3,2,1,0:T(8,128)(2,1)}), bf16[32,2,64,128]{3,2,1,0:T(8,128)(2,1)S(1)}, u32[]{:S(2)}, u32[]{:S(2)}) async-start(bf16[32,2,64,128]{3,2,1,0:T(8,128)(2,1)} %broadcast_select_fusion), calls=%async_computation.1 | async-start | bytes 2097152 | tf_op jit(solution)/shard_map/all_to_all | solution.py:124
  167.2 243.9 %collective-permute-start.1 = (bf16[32,64,128]{2,1,0:T(8,128)(2,1)}, bf16[32,64,128]{2,1,0:T(8,128)(2,1)S(1)}, u32[]{:S(2)}, u32[]{:S(2)}) collective-permute-start(bf16[32,64,128]{2,1,0:T(8,128)(2,1)} %bitcast.17), channel_id=1, source_target_pairs={{0,224},{32,0},{64,32},{96,64},{128,96},{160,128},{192,160},{224,1... | collective-permute-start | bytes 1572872 | tf_op jit(solution)/shard_map/ppermute | solution.py:20
  442.3 0.8 copy-start

commit v2 on v1

--- a/solution.py
+++ b/solution.py
@@ -5,19 +5,12 @@
 from jax.experimental.pallas import tpu as pltpu
 from jax.sharding import PartitionSpec as P
 
-HEADS = 32
 DIM = 64
-BLOCKS = 32
 ROWS = 64
 EPS = 1e-06
 F32 = jnp.float32
 BF16 = jnp.bfloat16
-
-
-def from_behind(value, axis, steps):
-    count = lax.axis_size(axis)
-    pairs = [(source, (source + steps) % count) for source in range(count)]
-    return lax.ppermute(value, axis, pairs)
+MESH = pl.DeviceIdType.MESH
 
 
 def dims_by_tokens(pairs):
@@ -75,56 +68,203 @@
     return rows_of_pairs(attended).astype(BF16), jnp.concatenate([query_col, key_col], axis=0)
 
 
-def attention_kernel(qkv_ref, grad_ref, other_ref, gain_ref, live_ref, out_ref, gain_out_ref):
+def step_offset(step):
+    return ((step + 1) // 2) * (2 * (step % 2) - 1)
+
+
+def relay_kernel(
+    table_ref, gain_ref, qkv_ref, grad_ref, out_ref, sums_ref,
+    own_qkv, own_grad, held, picked, others, notes_out, notes,
+    terms_out, terms, totals_out, totals,
+    own_send, own_recv, grad_send, grad_recv, held_send, held_recv,
+    other_send, other_recv, note_send, note_recv,
+    term_send, term_recv, total_send, total_recv,
+):
+    n = held.shape[0]
+    replicas = totals.shape[0]
+    stages = lax.axis_size("pipe")
+    d, p, z = lax.axis_index("dp"), lax.axis_index("pipe"), lax.axis_index("ctx")
+    ahead = lax.rem(p + 1, stages)
+    behind = lax.rem(p + stages - 1, stages)
+
+    def partner(step):
+        return lax.rem(z + step_offset(step) + n, n)
+
+    def remote(src, dst, send, recv, target):
+        return pltpu.make_async_remote_copy(
+            src_ref=src, dst_ref=dst, send_sem=send, recv_sem=recv,
+            device_id=target, device_id_type=MESH,
+        )
+
+    barrier = pltpu.get_barrier_semaphore()
+
+    def greet(step, carry):
+        other = partner(step)
+        pl.semaphore_signal(barrier, inc=1, device_id=(d, ahead, other), device_id_type=MESH)
+        pl.semaphore_signal(barrier, inc=1, device_id=(d, behind, other), device_id_type=MESH)
+
+        @pl.when(step > 0)
+        def _():
+            pl.semaphore_signal(barrier, inc=1, device_id=(d, p, other), device_id_type=MESH)
+
+        return carry
+
+    lax.fori_loop(0, n, greet, 0)
+    for hop in range(1, replicas):
+        pl.semaphore_signal(
+            barrier, inc=1, device_id=(lax.rem(d + hop, replicas), p, z), device_id_type=MESH
+        )
+
+    def write_note(block, carry):
+        live = jnp.where(table_ref[2 * block + 1] < n, 1.0, 0.0).astype(F32)
+        notes_out[block, 0:1, :] = gain_ref[...]
+        notes_out[block, 1:2, :] = jnp.full((1, 128), live, F32)
+        return carry
+
+    lax.fori_loop(0, n, write_note, 0)
+    notes[z] = notes_out[z]
+    pl.semaphore_wait(barrier, 3 * n - 1 + replicas - 1)
+
+    def send_note(step, carry):
+        other = partner(step)
+        remote(notes_out.at[other], notes.at[z], note_send, note_recv, (d, p, other)).start()
+        return carry
+
+    def send_to_owner(step, carry):
+        other = partner(step)
+        remote(
+            qkv_ref.at[pl.ds(1, 2), other], held.at[z], held_send, held_recv, (d, ahead, other)
+        ).start()
+        return carry
+
+    lax.fori_loop(1, n, send_note, 0)
+    lax.fori_loop(0, n, send_to_owner, 0)
+    own_copy = remote(qkv_ref, own_qkv, own_send, own_recv, (d, ahead, z))
+    own_copy.start()
+    grad_copy = remote(grad_ref, own_grad, grad_send, grad_recv, (d, behind, z))
+    grad_copy.start()
+
+    all_held = remote(held, held, held_send, held_recv, (d, ahead, z))
+    all_held.wait_recv()
+
+    def pick(block):
+        listed = table_ref[2 * block + 1]
+        return held[jnp.where(listed < n, listed, 0)]
+
+    others[z] = pick(z)
+
+    def send_picked(step, carry):
+        other = partner(step)
+        picked[other] = pick(other)
+        remote(
+            picked.at[other], others.at[z], other_send, other_recv.at[z], (d, p, other)
+        ).start()
+        return carry
+
+    lax.fori_loop(1, n, send_picked, 0)
+    own_copy.wait_recv()
+    grad_copy.wait_recv()
+    rest = pl.ds(0, n - 1)
+    all_notes = remote(notes_out.at[rest], notes.at[rest], note_send, note_recv, (d, p, z))
+    all_notes.wait_recv()
     lane = lax.broadcasted_iota(jnp.int32, (2 * DIM, 128), 1)
 
-    def step(head, totals):
+    def attend(step, sums):
+        head = partner(step)
+
+        @pl.when(step > 0)
+        def _():
+            remote(
+                picked.at[head], others.at[head], other_send, other_recv.at[head], (d, p, head)
+            ).wait_recv()
+
         out, col = one_head(
-            qkv_ref[0, head],
-            qkv_ref[1, head],
-            qkv_ref[2, head],
-            grad_ref[head],
-            other_ref[head, 0],
-            other_ref[head, 1],
-            gain_ref[head],
-            live_ref[head],
+            own_qkv[0, head], own_qkv[1, head], own_qkv[2, head], own_grad[head],
+            others[head, 0], others[head, 1], notes[head, 0:1, :], notes[head, 1:2, :],
         )
         out_ref[head] = out
-        return jnp.where(lane == head, col, totals)
-
-    totals = lax.fori_loop(0, HEADS, step, jnp.zeros((2 * DIM, 128), F32))
-    gain_out_ref[...] = totals.T[:HEADS]
-
-
-def attention(qkv, grads, others, gains, live):
+        return jnp.where(lane == head, col, sums)
+
+    sums = lax.fori_loop(0, n, attend, jnp.zeros((2 * DIM, 128), F32)).T
+    for head in range(n):
+        terms_out[head] = sums[head : head + 1]
+    terms[z] = terms_out[z]
+
+    def send_terms(step, carry):
+        other = partner(step)
+        remote(terms_out.at[other], terms.at[z], term_send, term_recv, (d, p, other)).start()
+        return carry
+
+    lax.fori_loop(1, n, send_terms, 0)
+    all_terms = remote(terms_out.at[rest], terms.at[rest], term_send, term_recv, (d, p, z))
+    all_terms.wait_recv()
+    total = jnp.sum(terms[...], axis=0)
+    totals[d] = total
+    totals_out[...] = total
+    for hop in range(1, replicas):
+        remote(
+            totals_out, totals.at[d], total_send, total_recv,
+            (lax.rem(d + hop, replicas), p, z),
+        ).start()
+    rows = pl.ds(0, replicas - 1)
+    all_totals = remote(totals.at[rows], totals.at[rows], total_send, total_recv, (d, p, z))
+    all_totals.wait_recv()
+    sums_ref[...] = jnp.sum(totals[...], axis=0)
+    own_copy.wait_send()
+    grad_copy.wait_send()
+    all_held.wait_send()
+    all_notes.wait_send()
+    remote(picked.at[rest], picked.at[rest], other_send, other_recv.at[z], (d, p, z)).wait_send()
+    all_terms.wait_send()
+    all_totals.wait_send()
+
+
+def relay(table, gains, qkv, grads):
+    n = grads.shape[0]
+    replicas = lax.axis_size("dp")
+    dma = pltpu.SemaphoreType.DMA
+    block = (ROWS, 128)
+    vmem = pl.BlockSpec(memory_space=pltpu.VMEM)
     return pl.pallas_call(
-        attention_kernel,
+        relay_kernel,
         out_shape=(
-            jax.ShapeDtypeStruct((HEADS, ROWS, 128), BF16),
-            jax.ShapeDtypeStruct((HEADS, 128), F32),
-        ),
-        in_specs=[pl.BlockSpec(memory_space=pltpu.VMEM)] * 5,
-        out_specs=(pl.BlockSpec(memory_space=pltpu.VMEM),) * 2,
-        compiler_params=pltpu.CompilerParams(vmem_limit_bytes=24 * 2**20),
-    )(qkv, grads, others, gains, live)
+            jax.ShapeDtypeStruct((n,) + block, BF16),
+            jax.ShapeDtypeStruct((1, 128), F32),
+        ),
+        in_specs=[pl.BlockSpec(memory_space=pltpu.SMEM), vmem, vmem, vmem],
+        out_specs=(vmem, vmem),
+        scratch_shapes=[
+            pltpu.VMEM((3, n) + block, BF16),
+            pltpu.VMEM((n,) + block, BF16),
+            pltpu.VMEM((n, 2) + block, BF16),
+            pltpu.VMEM((n, 2) + block, BF16),
+            pltpu.VMEM((n, 2) + block, BF16),
+            pltpu.VMEM((n, 2, 128), F32),
+            pltpu.VMEM((n, 2, 128), F32),
+            pltpu.VMEM((n, 1, 128), F32),
+            pltpu.VMEM((n, 1, 128), F32),
+            pltpu.VMEM((1, 128), F32),
+            pltpu.VMEM((replicas, 1, 128), F32),
+            dma, dma, dma, dma, dma, dma,
+            dma, dma((n,)), dma, dma,
+            dma, dma, dma, dma,
+        ],
+        compiler_params=pltpu.CompilerParams(
+            collective_id=0, has_side_effects=True, vmem_limit_bytes=32 * 2**20
+        ),
+        cost_estimate=pl.CostEstimate(
+            flops=n * 10 * 128 * 256 * DIM, bytes_accessed=n * 10 * 2**14,
+            transcendentals=n * 256 * 128,
+        ),
+    )(table, gains, qkv, grads)
 
 
 def local(activations, cotangents, norm_gains, key_blocks):
-    qkv = from_behind(activations[0, 0].reshape(3, HEADS, ROWS, 128), "pipe", 1)
-    grads = from_behind(cotangents[0, 0].reshape(HEADS, ROWS, 128), "pipe", -1)
-    table = key_blocks[0, 0]
-    gain_rows = lax.all_gather(norm_gains[0].reshape(1, 1, 128), "ctx", axis=0, tiled=True)
-    lists = lax.all_gather(table[None, :, 1], "ctx", axis=0, tiled=True)
-    live = (lists[:, lax.axis_index("ctx")] < BLOCKS).astype(F32)
-    live_rows = jnp.broadcast_to(live[:, None, None], (HEADS, 1, 128))
-    keys_values = jnp.swapaxes(qkv[1:], 0, 1)
-    held = lax.all_to_all(keys_values, "ctx", split_axis=0, concat_axis=0, tiled=True)
-    listed = jnp.where(table[:, 1] < BLOCKS, table[:, 1], 0)
-    picked = jnp.take(held, listed, axis=0)
-    others = lax.all_to_all(picked, "ctx", split_axis=0, concat_axis=0, tiled=True)
-    out, terms = attention(qkv, grads, others, gain_rows, live_rows)
-    summed = lax.psum(lax.psum_scatter(terms, "ctx", scatter_dimension=0, tiled=True), "dp")
-    return out.reshape(1, 1, HEADS, ROWS * 128), summed.reshape(1, 2, 1, DIM)
+    heads = activations.shape[3]
+    qkv = activations.reshape(3, heads, ROWS, 128)
+    grads = cotangents.reshape(heads, ROWS, 128)
+    out, sums = relay(key_blocks.reshape(-1), norm_gains.reshape(1, 128), qkv, grads)
+    return out.reshape(1, 1, heads, ROWS * 128), sums.reshape(1, 2, 1, DIM)
 
 
 def solution(mesh):

time: 566 us -> 260 us (0.46)
  blocking collectives: 355 us -> 0 us
  Pallas kernels: 31.1 us -> 248 us
  waiting for transfers between devices: 123 us -> 0 us
  starting transfers between devices: 36.9 us -> 0 us
  local copies, waits for them, and re-layouts: 11.9 us -> 6.11 us
    unnamed x2 -> x0, blocking collectives: 292 us -> none
    pallas_call x1, Pallas kernels: 31.1 us -> 248 us  [relay(): pl.pallas_call(relay_kernel, out_shape=(jax.ShapeDtypeStruct((n,) + block...]
    all_to_all x2 -> x0, waiting for transfers between devices: 104 us -> none  [the longest x1 104 us: local(): lax.all_to_all(keys_values, 'ctx', split_axis=0, concat_axis=0, tiled=True)]
    all_gather x1 -> x0, blocking collectives: 52.8 us -> none  [local(): lax.all_gather(norm_gains[0].reshape(1, 1, 128), 'ctx', axis=0, tiled=True)]
    all_to_all x2 -> x0, starting transfers between devices: 35.9 us -> none  [the longest x1 29 us: local(): lax.all_to_all(keys_values, 'ctx', split_axis=0, concat_axis=0, tiled=True)]
    ppermute x2 -> x0, waiting for transfers between devices: 19.8 us -> none  [from_behind(): return lax.ppermute(value, axis, pairs)]
    psum x1 -> x0, blocking collectives: 11 us -> none  [local(): lax.psum(lax.psum_scatter(terms, 'ctx', scatter_dimension=0, tiled=True),...]
  transfers between devices with their start and end apart: 4 -> 0, of which waited for: 2 -> 0; matrix products, arithmetic and copies ran while one was open for 1% -> 0% of each run, Pallas kernels for 0% -> 0%
where the time goes in v2:
time: 260 us; the launch traced here: 256 us
  Pallas kernels  248 us (95%)
  local copies, waits for them, and re-layouts  6.11 us (2%)
    pallas_call x1, Pallas kernels, relay(): pl.pallas_call(relay_kernel, out_shape=(jax.ShapeDtypeStruct((n,) + block...  248 us

profile of v2, /device:TPU:24, one launch (start us, length us, event | category | flops | bytes accessed | tf_op | source)
XLA Modules:
  0.0 256.3 jit_solution(8607795774234231114)
XLA Ops:
  0.6 0.5 broadcast.6
  1.1 1.3 reduce.6
  2.5 0.1 reshape.23.gain_ref
  2.6 0.8 copy.8
  3.3 0.1 reshape.22.table_ref
  3.4 1.2 copy.11
  4.6 1.8 copy.10
  6.4 247.5 %shard_map.59 = (bf16[32,64,128]{2,1,0:T(8,128)(2,1)S(1)}, f32[1,128]{1,0:T(1,128)S(1)}) custom-call(s32[64]{0:T(128)S(1)} %reshape.22.table_ref, f32[1,128]{1,0:T(1,128)S(1)} %reshape.23.gain_ref, bf16[3,32,64,128]{3,2,1,0:T(8,128)(2,1)S(1)} %bitcast.12, bf16[32,64,128]{2,1,0:T(8,128)(2,1)S(1)} %bitcast.13), custom_call_target="tpu_custom_call" | custom-call | flops 671088640 | bytes 5242880 | tf_op jit(solution)/shard_map/pallas_call | solution.py:228
  254.0 1.0 reshape.26
  255.0 0.7 reduce.7
  255.7 0.6 reshape.27

commit v3 on v2

v3 whole, which is shorter than its diff:
```python
import jax
import jax.numpy as jnp
from jax import lax
from jax.experimental import pallas as pl
from jax.experimental.pallas import tpu as pltpu
from jax.sharding import PartitionSpec as P

DIM = 64
SCALE = DIM ** (-0.5)
ROWS = 64
EPS = 1e-06
F32 = jnp.float32
BF16 = jnp.bfloat16
MESH = pl.DeviceIdType.MESH


def dims_by_tokens(pairs):
    turned = pairs.astype(F32).T
    return jnp.concatenate([turned[:DIM], turned[DIM:]], axis=1)


def rows_of_pairs(turned):
    return jnp.concatenate([turned[:, :DIM], turned[:, DIM:]], axis=0).T


def contract(left, right, left_dim, right_dim):
    return lax.dot_general(
        left, right, (((left_dim,), (right_dim,)), ((), ())), preferred_element_type=F32
    )


def unit(vals):
    return vals * lax.rsqrt(jnp.mean(vals * vals, axis=0, keepdims=True) + EPS)


def prepare_head(query, key, value, grad, gain_row):
    gains = jnp.broadcast_to(gain_row, (2 * DIM, 2 * DIM)).T
    q_unit = unit(dims_by_tokens(query))
    k_unit = unit(dims_by_tokens(key))
    q_normed = (q_unit * gains[:DIM]).astype(BF16)
    k_normed = (k_unit * gains[DIM:]).astype(BF16)
    values = dims_by_tokens(value).astype(BF16)
    grad_t = dims_by_tokens(grad).astype(BF16)
    scores = contract(k_normed, q_normed, 0, 0) * SCALE
    grad_probs = contract(values, grad_t, 0, 0)
    return q_unit, k_unit, gains[DIM:], q_normed, k_normed, values, grad_t, scores, grad_probs


def weigh_head(other_key, key_gain, q_normed, own_scores, own_values, live_row):
    o_unit = unit(dims_by_tokens(other_key))
    o_normed = (o_unit * key_gain).astype(BF16)
    other_scores = contract(o_normed, q_normed, 0, 0) * SCALE
    other_scores = jnp.where(live_row > 0.5, other_scores, -jnp.inf)
    row_max = jnp.maximum(
        jnp.max(own_scores, axis=0, keepdims=True), jnp.max(other_scores, axis=0, keepdims=True)
    )
    exp_own = jnp.exp(own_scores - row_max)
    exp_other = jnp.exp(other_scores - row_max)
    row_sum = jnp.sum(exp_own, axis=0, keepdims=True) + jnp.sum(exp_other, axis=0, keepdims=True)
    own_probs, other_probs = exp_own / row_sum, exp_other / row_sum
    own_part = contract(own_values, own_probs.astype(BF16), 1, 0)
    return o_unit, o_normed, own_probs, other_probs, own_part


def finish_head(
    other_value, q_unit, k_unit, o_unit, q_normed, k_normed, o_normed,
    grad_t, own_grad_probs, own_probs, other_probs, own_part,
):
    values = dims_by_tokens(other_value).astype(BF16)
    attended = own_part + contract(values, other_probs.astype(BF16), 1, 0)
    grad_probs = contract(values, grad_t, 0, 0)
    row_dot = jnp.sum(grad_t.astype(F32) * attended, axis=0, keepdims=True)
    own_terms = (own_probs * (own_grad_probs - row_dot) * SCALE).astype(BF16)
    other_terms = (other_probs * (grad_probs - row_dot) * SCALE).astype(BF16)
    grad_query = contract(k_normed, own_terms, 1, 0) + contract(o_normed, other_terms, 1, 0)
    grad_key = contract(q_normed, own_terms, 1, 1)
    grad_other = contract(q_normed, other_terms, 1, 1)
    sums = jnp.concatenate([grad_query * q_unit, grad_key * k_unit + grad_other * o_unit], axis=0)
    return rows_of_pairs(attended).astype(BF16), jnp.sum(sums.T, axis=0, keepdims=True)


def step_offset(step):
    return ((step + 1) // 2) * (2 * (step % 2) - 1)


def relay_kernel(
    table_ref, gain_ref, qkv_rows, grad_rows, out_ref, sums_ref, qkv_ref, grad_ref,
    own_qkv, own_grad, held_keys, held_values, picked, others, notes_out, notes,
    terms_out, terms, totals_out, totals,
    own_send, own_recv, grad_send, grad_recv, held_send, held_recv,
    other_send, other_recv, note_send, note_recv,
    term_send, term_recv, total_send, total_recv,
    units, gains, normed, own_scores, own_grad_probs, probs, parts,
):
    n = held_keys.shape[0]
    replicas = totals.shape[0]
    stages = lax.axis_size("pipe")
    d, p, z = lax.axis_index("dp"), lax.axis_index("pipe"), lax.axis_index("ctx")
    ahead = lax.rem(p + 1, stages)
    behind = lax.rem(p + stages - 1, stages)

    def partner(step):
        return lax.rem(z + step_offset(step) + n, n)

    def remote(src, dst, send, recv, target):
        return pltpu.make_async_remote_copy(
            src_ref=src, dst_ref=dst, send_sem=send, recv_sem=recv,
            device_id=target, device_id_type=MESH,
        )

    barrier = pltpu.get_barrier_semaphore()

    def greet(step, carry):
        other = partner(step)
        pl.semaphore_signal(barrier, inc=1, device_id=(d, ahead, other), device_id_type=MESH)
        pl.semaphore_signal(barrier, inc=1, device_id=(d, behind, other), device_id_type=MESH)

        @pl.when(step > 0)
        def _():
            pl.semaphore_signal(barrier, inc=1, device_id=(d, p, other), device_id_type=MESH)

        return carry

    lax.fori_loop(0, n, greet, 0)
    for hop in range(1, replicas):
        pl.semaphore_signal(
            barrier, inc=1, device_id=(lax.rem(d + hop, replicas), p, z), device_id_type=MESH
        )

    width = 16 * 128

    def split_rows(index, carry):
        field, part = index // 4, lax.rem(index, 4)
        columns = pl.ds(pl.multiple_of(part * width, width), width)
        rows = pl.ds(pl.multiple_of(part * 16, 16), 16)
        qkv_ref[field, :, rows] = qkv_rows[0, 0, field, :, columns].reshape(n, 16, 128)
        return carry

    def split_grad_rows(part, carry):
        columns = pl.ds(pl.multiple_of(part * width, width), width)
        rows = pl.ds(pl.multiple_of(part * 16, 16), 16)
        grad_ref[:, rows] = grad_rows[0, 0, :, columns].reshape(n, 16, 128)
        return carry

    lax.fori_loop(0, 12, split_rows, 0)
    lax.fori_loop(0, 4, split_grad_rows, 0)
    gain_row = jnp.concatenate([gain_ref[0, 0], gain_ref[0, 1]], axis=1)

    def write_note(block, carry):
        live = jnp.where(table_ref[1, block] < n, 1.0, 0.0).astype(F32)
        notes_out[block, 0:1, :] = gain_row
        notes_out[block, 1:2, :] = jnp.full((1, 128), live, F32)
        return carry

    lax.fori_loop(0, n, write_note, 0)
    notes[z] = notes_out[z]
    pl.semaphore_wait(barrier, 3 * n - 1 + replicas - 1)

    def send_note(step, carry):
        other = partner(step)
        remote(notes_out.at[other], notes.at[z], note_send, note_recv, (d, p, other)).start()
        return carry

    held = (held_keys, held_values)

    def send_to_owner(field):
        def send(index, carry):
            other = partner(n - 1 - index)
            remote(
                qkv_ref.at[1 + field, other], held[field].at[z],
                held_send.at[field], held_recv.at[field], (d, ahead, other),
            ).start()
            return carry

        lax.fori_loop(0, n, send, 0)

    lax.fori_loop(1, n, send_note, 0)
    send_to_owner(0)
    send_to_owner(1)
    own_copy = remote(qkv_ref, own_qkv, own_send, own_recv, (d, ahead, z))
    own_copy.start()
    grad_copy = remote(grad_ref, own_grad, grad_send, grad_recv, (d, behind, z))
    grad_copy.start()
    arrivals = [
        remote(held[field], held[field], held_send.at[field], held_recv.at[field], (d, ahead, z))
        for field in range(2)
    ]

    def pick(field, block):
        listed = table_ref[1, block]
        return held[field][jnp.where(listed < n, listed, 0)]

    def send_picked(field):
        def send(index, carry):
            other = partner(lax.rem(n - index, n))
            picked[other, field] = pick(field, other)
            remote(
                picked.at[other, field], others.at[z, field],
                other_send, other_recv.at[field, z], (d, p, other),
            ).start()
            return carry

        arrivals[field].wait_recv()
        lax.fori_loop(1, n, send, 0)
        others[z, field] = pick(field, z)

    send_picked(0)
    own_copy.wait_recv()
    grad_copy.wait_recv()
    rest = pl.ds(0, n - 1)
    all_notes = remote(notes_out.at[rest], notes.at[rest], note_send, note_recv, (d, p, z))
    all_notes.wait_recv()

    def prepare(head, carry):
        (
            units[head, 0], units[head, 1], gains[head],
            normed[head, 0], normed[head, 1], normed[head, 3], normed[head, 4],
            own_scores[head], own_grad_probs[head],
        ) = prepare_head(
            own_qkv[0, head], own_qkv[1, head], own_qkv[2, head], own_grad[head],
            notes[head, 0:1, :],
        )
        return carry

    lax.fori_loop(0, n, prepare, 0)
    send_picked(1)

    def landed(field, head):
        remote(
            picked.at[head, field], others.at[head, field],
            other_send, other_recv.at[field, head], (d, p, head),
        ).wait_recv()

    def weigh(index, carry):
        head = partner(lax.rem(n - index, n))

        @pl.when(index > 0)
        def _():
            landed(0, head)

        units[head, 2], normed[head, 2], probs[head, 0], probs[head, 1], parts[head] = weigh_head(
            others[head, 0], gains[head], normed[head, 0], own_scores[head], normed[head, 3],
            notes[head, 1:2, :],
        )
        return carry

    lax.fori_loop(0, n, weigh, 0)

    def finish(index, carry):
        head = partner(lax.rem(n - index, n))

        @pl.when(index > 0)
        def _():
            landed(1, head)

        out_ref[head], terms_out[head] = finish_head(
            others[head, 1], units[head, 0], units[head, 1], units[head, 2],
            normed[head, 0], normed[head, 1], normed[head, 2], normed[head, 4],
            own_grad_probs[head], probs[head, 0], probs[head, 1], parts[head],
        )

        @pl.when(index > 0)
        def _():
            remote(terms_out.at[head], terms.at[z], term_send, term_recv, (d, p, head)).start()

        return carry

    lax.fori_loop(0, n, finish, 0)
    terms[z] = terms_out[z]
    all_terms = remote(terms_out.at[rest], terms.at[rest], term_send, term_recv, (d, p, z))
    all_terms.wait_recv()
    total = jnp.sum(terms[...], axis=0)
    totals[d] = total
    totals_out[...] = total
    for hop in range(1, replicas):
        remote(
            totals_out, totals.at[d], total_send, total_recv,
            (lax.rem(d + hop, replicas), p, z),
        ).start()
    rows = pl.ds(0, replicas - 1)
    all_totals = remote(totals.at[rows], totals.at[rows], total_send, total_recv, (d, p, z))
    all_totals.wait_recv()
    result = jnp.sum(totals[...], axis=0)
    sums_ref[0, 0] = result[:, :DIM]
    sums_ref[0, 1] = result[:, DIM:]
    own_copy.wait_send()
    grad_copy.wait_send()
    arrivals[0].wait_send()
    arrivals[1].wait_send()
    all_notes.wait_send()
    remote(picked.at[rest], picked.at[rest], other_send, other_recv.at[0, z], (d, p, z)).wait_send()
    all_terms.wait_send()
    all_totals.wait_send()


def relay(table, gains, qkv, grads):
    n = grads.shape[2]
    replicas = lax.axis_size("dp")
    dma = pltpu.SemaphoreType.DMA
    block = (ROWS, 128)
    vmem = pl.BlockSpec(memory_space=pltpu.VMEM)
    return pl.pallas_call(
        relay_kernel,
        out_shape=(
            jax.ShapeDtypeStruct((n,) + block, BF16),
            jax.ShapeDtypeStruct((1, 2, 1, DIM), F32),
        ),
        in_specs=[pl.BlockSpec(memory_space=pltpu.SMEM), vmem, vmem, vmem],
        out_specs=(vmem, vmem),
        scratch_shapes=[
            pltpu.VMEM((3, n) + block, BF16),
            pltpu.VMEM((n,) + block, BF16),
            pltpu.VMEM((3, n) + block, BF16),
            pltpu.VMEM((n,) + block, BF16),
            pltpu.VMEM((n,) + block, BF16),
            pltpu.VMEM((n,) + block, BF16),
            pltpu.VMEM((n, 2) + block, BF16),
            pltpu.VMEM((n, 2) + block, BF16),
            pltpu.VMEM((n, 2, 128), F32),
            pltpu.VMEM((n, 2, 128), F32),
            pltpu.VMEM((n, 1, 128), F32),
            pltpu.VMEM((n, 1, 128), F32),
            pltpu.VMEM((1, 128), F32),
            pltpu.VMEM((replicas, 1, 128), F32),
            dma, dma, dma, dma, dma((2,)), dma((2,)),
            dma, dma((2, n)), dma, dma,
            dma, dma, dma, dma,
            pltpu.VMEM((n, 3, DIM, 128), F32),
            pltpu.VMEM((n, DIM, 128), F32),
            pltpu.VMEM((n, 5, DIM, 128), BF16),
            pltpu.VMEM((n, 128, 128), F32),
            pltpu.VMEM((n, 128, 128), F32),
            pltpu.VMEM((n, 2, 128, 128), F32),
            pltpu.VMEM((n, DIM, 128), F32),
        ],
        compiler_params=pltpu.CompilerParams(
            collective_id=0, has_side_effects=True, vmem_limit_bytes=48 * 2**20
        ),
        cost_estimate=pl.CostEstimate(
            flops=n * 10 * 128 * 256 * DIM, bytes_accessed=n * 10 * 2**14,
            transcendentals=n * 256 * 128,
        ),
    )(table, gains, qkv, grads)


def local(activations, cotangents, norm_gains, key_blocks):
    heads = activations.shape[3]
    table = jnp.swapaxes(key_blocks[0, 0], 0, 1)
    out, sums = relay(table, norm_gains, activations, cotangents)
    return out.reshape(1, 1, heads, ROWS * 128), sums


def solution(mesh):
    return jax.shard_map(
        local,
        mesh=mesh,
        in_specs=(
            P("dp", "pipe", None, None, "ctx"),
            P("dp", "pipe", None, "ctx"),
            P("pipe", None, "ctx", None),
            P("pipe", "ctx", None, None),
        ),
        out_specs=(P("dp", "pipe", None, "ctx"), P("pipe", None, "ctx", None)),
        check_vma=False,
    )
```

time: 260 us -> 235 us (0.904); the launches traced: 256 us -> 234 us
  Pallas kernels: 248 us -> 228 us
    pallas_call x1, Pallas kernels: 248 us -> 228 us  [relay(): pl.pallas_call(relay_kernel, out_shape=(jax.ShapeDtypeStruct((n,) + block...]
where the time goes in v3:
time: 235 us; the launch traced here: 234 us
  Pallas kernels  228 us (97%)
  local copies, waits for them, and re-layouts  5.38 us (2%)
    pallas_call x1, Pallas kernels, relay(): pl.pallas_call(relay_kernel, out_shape=(jax.ShapeDtypeStruct((n,) + block...  228 us

profile of v3, /device:TPU:24, one launch (start us, length us, event | category | flops | bytes accessed | tf_op | source)
XLA Modules:
  0.0 234.1 jit_solution(910459433087108871)
XLA Ops:
  0.6 0.0 copy-start
  0.6 1.4 copy-done
  2.0 0.0 copy-start.1
  2.0 1.0 copy-done.1
  3.1 0.0 copy-start.2
  3.1 0.7 copy-done.2
  3.8 0.0 copy-start.3
  3.8 0.7 copy-done.3
  4.4 228.1 %shard_map.59 = (bf16[32,64,128]{2,1,0:T(8,128)(2,1)S(1)}, f32[1,2,1,64]{3,2,1,0:T(1,128)S(1)}) custom-call(s32[2,32]{1,0:T(2,128)S(1)} %bitcast.3, f32[1,2,1,64]{3,2,1,0:T(1,128)S(1)} %copy-done.3, bf16[1,1,3,32,8192]{4,3,2,1,0:T(8,128)(2,1)S(1)} %copy-done, bf16[1,1,32,8192]{3,2,1,0:T(8,128)(2,1)S(1)} %copy-done.1), custom_call_target="tpu_custom_call" | custom-call | flops 671088640 | bytes 5242880 | tf_op jit(solution)/shard_map/pallas_call | solution.py:302
  232.6 1.0 reshape.7
  233.6 0.6 copy.7
Async XLA Ops:
  0.6 1.4 copy-start
  2.0 1.0 copy-start.1
  3.1 0.7 copy-start.2
  3.8 0.7 copy-start.3

commit v4 on v3

--- a/solution.py
+++ b/solution.py
@@ -84,7 +84,8 @@
 
 
 def relay_kernel(
-    table_ref, gain_ref, qkv_rows, grad_rows, out_ref, sums_ref, qkv_ref, grad_ref,
+    table_ref, gain_hbm, qkv_hbm, grad_hbm, out_ref, sums_ref,
+    gain_ref, qkv_rows, grad_rows, in_sems, qkv_ref, grad_ref,
     own_qkv, own_grad, held_keys, held_values, picked, others, notes_out, notes,
     terms_out, terms, totals_out, totals,
     own_send, own_recv, grad_send, grad_recv, held_send, held_recv,
@@ -108,9 +109,18 @@
             device_id=target, device_id_type=MESH,
         )
 
+    inputs = [
+        pltpu.make_async_copy(src, dst, in_sems.at[index])
+        for index, (src, dst) in enumerate(
+            ((qkv_hbm, qkv_rows), (grad_hbm, grad_rows), (gain_hbm, gain_ref))
+        )
+    ]
+    for copy in inputs:
+        copy.start()
     barrier = pltpu.get_barrier_semaphore()
 
-    def greet(step, carry):
+    def greet(index, carry):
+        step = n - 1 - index
         other = partner(step)
         pl.semaphore_signal(barrier, inc=1, device_id=(d, ahead, other), device_id_type=MESH)
         pl.semaphore_signal(barrier, inc=1, device_id=(d, behind, other), device_id_type=MESH)
@@ -127,6 +137,8 @@
             barrier, inc=1, device_id=(lax.rem(d + hop, replicas), p, z), device_id_type=MESH
         )
 
+    for copy in inputs:
+        copy.wait()
     width = 16 * 128
 
     def split_rows(index, carry):
@@ -299,15 +311,20 @@
     dma = pltpu.SemaphoreType.DMA
     block = (ROWS, 128)
     vmem = pl.BlockSpec(memory_space=pltpu.VMEM)
+    hbm = pl.BlockSpec(memory_space=pl.ANY)
     return pl.pallas_call(
         relay_kernel,
         out_shape=(
             jax.ShapeDtypeStruct((n,) + block, BF16),
             jax.ShapeDtypeStruct((1, 2, 1, DIM), F32),
         ),
-        in_specs=[pl.BlockSpec(memory_space=pltpu.SMEM), vmem, vmem, vmem],
+        in_specs=[pl.BlockSpec(memory_space=pltpu.SMEM), hbm, hbm, hbm],
         out_specs=(vmem, vmem),
         scratch_shapes=[
+            pltpu.VMEM(gains.shape, F32),
+            pltpu.VMEM(qkv.shape, BF16),
+            pltpu.VMEM(grads.shape, BF16),
+            dma((3,)),
             pltpu.VMEM((3, n) + block, BF16),
             pltpu.VMEM((n,) + block, BF16),
             pltpu.VMEM((3, n) + block, BF16),
@@ -334,7 +351,7 @@
             pltpu.VMEM((n, DIM, 128), F32),
         ],
         compiler_params=pltpu.CompilerParams(
-            collective_id=0, has_side_effects=True, vmem_limit_bytes=48 * 2**20
+            collective_id=0, has_side_effects=True, vmem_limit_bytes=62 * 2**20
         ),
         cost_estimate=pl.CostEstimate(
             flops=n * 10 * 128 * 256 * DIM, bytes_accessed=n * 10 * 2**14,

time: 235 us -> 232 us (0.987)
    unnamed x9 -> x1, local copies, waits for them, and re-layouts: 4.36 us -> 1.2 us
where the time goes in v4:
time: 232 us
  Pallas kernels  228 us (98%)
  local copies, waits for them, and re-layouts  3.26 us (1%)
    pallas_call x1, Pallas kernels, relay(): pl.pallas_call(relay_kernel, out_shape=(jax.ShapeDtypeStruct((n,) + block...  228 us

profile of v4, /device:TPU:24, one launch (start us, length us, event | category | flops | bytes accessed | tf_op | source)
XLA Modules:
  0.0 231.9 jit_solution(1606903464910925050)
XLA Ops:
  0.6 228.0 %shard_map.59 = (bf16[32,64,128]{2,1,0:T(8,128)(2,1)}, f32[1,2,1,64]{3,2,1,0:T(1,128)}) custom-call(s32[2,32]{1,0:T(2,128)} %bitcast.3, f32[1,2,1,64]{3,2,1,0:T(1,128)} %gain_hbm.1, bf16[1,1,3,32,8192]{4,3,2,1,0:T(8,128)(2,1)} %qkv_hbm.1, bf16[1,1,32,8192]{3,2,1,0:T(8,128)(2,1)} %grad_hbm.1), custom_call_target="tpu_custom_call" | custom-call | flops 671088640 | bytes 5242880 | tf_op jit(solution)/shard_map/pallas_call | solution.py:315
  228.7 2.1 reshape.7
  230.7 1.2 copy.7
